TPU v7x, 32 devices: a whole 2x2x4 slice. The times are simulated.
32 devices in a mesh: cfg: 2 (over y), src: 8 (over z, core), snk: 2 (over x), spin: 1.
Axes of the slice: x: 2, y: 2, z: 4, core: 2. Of those that a mesh axis runs over, the one named last changes fastest.
Arguments:
- src_times: int32 [8], P('src'), may hold values from 0 to 31, as said below
- momenta: int32 [8, 2], P('src'), may hold values from 0 to 1
- band_offsets: int32 [16], P('snk'), may hold values from 0 to 15, as said below
- elementals: bfloat16 [4, 32, 2, 128, 128], P('cfg', 'src'), parts along dimension 0, may hold values from -0.5 to 0.5
- perambulators: bfloat16 [16, 16, 2, 512, 512], P(('cfg', 'src'), 'snk', None, None, 'spin'), parts along dimension 0, may hold values from -1.1953125 to 1.1953125
Outputs:
- trace_terms: float32 [16, 16, 2, 512], P(('cfg', 'src'), 'snk', None, 'spin'), parts along dimension 0
- correlator: float32 [16, 16, 2], P(('cfg', 'src'), 'snk'), parts along dimension 0
There are 2 independent parts, one for each index of `cfg`. A program takes and returns all parts, laid end to end along the dimension named above; an argument that names none is the same for every part. Nothing has to cross between parts.
Inputs may be any that keep to these rules, and one draw needn't show every extreme that they name: src_times[s] lies in [s * 4, (s + 1) * 4); the first and the last source sit at the last slice of their tile. `band_offsets`: each offset appears once.
All inputs are finite; a program needn't handle non-finite values.
Results may differ from a plain program's by a relative error of at most 0.014.
Values may be sent and summed in bfloat16 or wider, within the bound.
A program may use at most 128 MiB of HBM per device.

v0:
```python
import jax
import jax.numpy as jnp
from jax import lax
from jax.sharding import PartitionSpec as P

EIG = 128
ROWS = 512


def from_behind(value, axis, steps):
    count = lax.axis_size(axis)
    pairs = [(source, (source + steps) % count) for source in range(count)]
    return lax.ppermute(value, axis, pairs)


def contract(source_elem, sink_elem, tau):
    width = tau.shape[-1]
    blocks = tau.reshape(2, 4, EIG, width)

    def rowmul(a, b):
        return jnp.einsum("ab,pbc->pac", a, b, preferred_element_type=jnp.float32).reshape(
            4 * EIG, width
        )

    left_re = (rowmul(source_elem[0], blocks[0]) - rowmul(source_elem[1], blocks[1])).astype(
        jnp.bfloat16
    )
    left_im = (rowmul(source_elem[0], blocks[1]) + rowmul(source_elem[1], blocks[0])).astype(
        jnp.bfloat16
    )
    columns = tau.reshape(2, 4 * EIG, width // EIG, EIG)

    def colmul(a, b):
        return jnp.einsum("ab,iqb->qai", a, b, preferred_element_type=jnp.float32).reshape(
            width, 4 * EIG
        )

    right_re = (colmul(sink_elem[0], columns[0]) + colmul(sink_elem[1], columns[1])).astype(
        jnp.bfloat16
    )
    right_im = (colmul(sink_elem[1], columns[0]) - colmul(sink_elem[0], columns[1])).astype(
        jnp.bfloat16
    )
    lre = left_re.astype(jnp.float32)
    lim = left_im.astype(jnp.float32)
    rre = right_re.astype(jnp.float32)
    rim = right_im.astype(jnp.float32)
    real_part = jnp.sum(lre * rre.T - lim * rim.T, axis=0)
    imag_part = jnp.sum(lre * rim.T + lim * rre.T, axis=0)
    return jnp.stack([real_part, imag_part])


def local(src_times, momenta, band_offsets, elementals, perambulators):
    tile = elementals.shape[1]
    first_slice = lax.axis_index("src") * tile
    start = src_times[0] - first_slice
    band_total = band_offsets.shape[0] * lax.axis_size("snk")
    reach = band_total // tile
    source_elem = elementals[momenta[0, 0], start]
    pieces = [elementals]
    for step in range(1, reach + 1):
        pieces.append(from_behind(elementals, "src", -step))
    window = jnp.concatenate(pieces, axis=1)[momenta[0, 1]]
    positions = start + band_offsets
    selector = (positions[:, None] == jnp.arange(window.shape[0], dtype=jnp.int32)[None, :]).astype(
        jnp.bfloat16
    )
    sink_elem = jnp.einsum(
        "ow,wxab->oxab", selector, window, preferred_element_type=jnp.float32
    ).astype(jnp.bfloat16)
    terms = jax.vmap(contract, in_axes=(None, 0, 0))(source_elem, sink_elem, perambulators[0])
    partial_sum = jnp.sum(terms, axis=-1)
    total = lax.psum(partial_sum, "spin")
    correlator = total * jnp.float32(ROWS ** (-0.5))
    return (terms[None], correlator[None])


def solution(mesh):
    placed = (
        P("src"),
        P("src", None),
        P("snk"),
        P("cfg", "src", None, None, None),
        P(("cfg", "src"), "snk", None, None, "spin"),
    )
    return jax.shard_map(
        local,
        mesh=mesh,
        in_specs=placed,
        out_specs=(P(("cfg", "src"), "snk", None, "spin"), P(("cfg", "src"), "snk", None)),
        check_vma=False,
    )
```

profile of v0, /device:TPU:0, one launch (start us, length us, event | category | flops | bytes accessed | tf_op | source)
XLA Modules:
  0.0 115.2 jit_solution(3562499333360690070)
XLA Ops:
  0.6 4.5 %collective-permute-start = (bf16[2,4,2,128,128]{4,3,2,1,0:T(8,128)(2,1)}, bf16[2,4,2,128,128]{4,3,2,1,0:T(8,128)(2,1)S(1)}, u32[]{:S(2)}, u32[]{:S(2)}) collective-permute-start(bf16[2,4,2,128,128]{4,3,2,1,0:T(8,128)(2,1)} %param.8), channel_id=1, source_target_pairs={{0,14},{2,0},{4,2},{6,4},{8,6},{10,8},{12,10},{14,12},{1,15},{3,1}... | collective-permute-start | bytes 1572872 | tf_op jit(solution)/shard_map/ppermute | solution.py:13
  5.2 0.6 collective-permute-start.1
  5.8 2.7 %collective-permute-start.3 = (bf16[2,4,2,128,128]{4,3,2,1,0:T(8,128)(2,1)}, bf16[2,4,2,128,128]{4,3,2,1,0:T(8,128)(2,1)S(1)}, u32[]{:S(2)}, u32[]{:S(2)}) collective-permute-start(bf16[2,4,2,128,128]{4,3,2,1,0:T(8,128)(2,1)} %param.8), channel_id=1, source_target_pairs={{0,8},{2,10},{4,12},{6,14},{8,0},{10,2},{12,4},{14,6},{1,9},{3,11}... | collective-permute-start | bytes 1572872 | tf_op jit(solution)/shard_map/ppermute | solution.py:13
  9.1 1.3 %fusion.32 = (s32[1,1]{1,0:T(1,128)}, s32[1,1]{1,0:T(1,128)}) fusion(s32[1,2]{1,0:T(1,128)} %param.6), kind=kLoop, calls=%fused_computation.56 | loop fusion | bytes 16 | tf_op jit(solution)/shard_map/slice | solution.py:63
  11.8 7.4 %copy.26 = bf16[1,8,2,512,512]{4,3,1,2,0:T(8,128)(2,1)} copy(bf16[1,8,2,512,512]{4,3,2,1,0:T(8,128)(2,1)} %param.9) | data formatting | bytes 16777216 | tf_op args[4]
  19.9 3.6 %fusion.7 = f32[128,8,4,512]{3,0,2,1:T(8,128)S(1)} fusion(bf16[8,2,4,128,512]{4,3,2,0,1:T(8,128)(2,1)} %bitcast.118, bf16[2,4,2,128,128]{4,3,2,1,0:T(8,128)(2,1)S(1)} %copy-done.2, s32[]{:T(128)S(6)} %select_n.9, s32[]{:T(128)S(6)} %select_n.10), kind=kOutput, calls=%fused_computation.19 | convolution fusion | flops 536870912 | bytes 12615688 | tf_op jit(solution)/shard_map/vmap(ab,pbc->pac)/dot_general | solution.py:21
  23.4 1.0 copy-done.1
  24.5 3.3 %subtract_convert_fusion.1 = bf16[128,8,4,512]{3,0,2,1:T(8,128)(2,1)} fusion(f32[128,8,4,512]{3,0,2,1:T(8,128)S(1)} %fusion.7, bf16[8,2,4,128,512]{4,3,2,0,1:T(8,128)(2,1)S(1)} %bitcast.120, bf16[2,4,2,128,128]{4,3,2,1,0:T(8,128)(2,1)S(1)} %copy-done.2, s32[]{:T(128)S(6)} %select_n.9, s32[]{:T(128)S(6)} %select_n.10, s32[]{:T(128)S(6)} %add.37), kind=kOutput, calls=%fused_computation.11 | convolution fusion | flops 541065216 | bytes 16809996 | tf_op jit(solution)/shard_map/vmap(ab,pbc->pac)/dot_general | solution.py:21
  27.8 4.5 %fusion.6 = f32[128,8,4,512]{3,0,2,1:T(8,128)} fusion(bf16[8,2,4,128,512]{4,3,2,0,1:T(8,128)(2,1)S(1)} %bitcast.121, bf16[2,4,2,128,128]{4,3,2,1,0:T(8,128)(2,1)S(1)} %copy-done.2, s32[]{:T(128)S(6)} %select_n.9, s32[]{:T(128)S(6)} %select_n.10, s32[]{:T(128)S(6)} %add.37), kind=kOutput, calls=%fused_computation.18 | convolution fusion | flops 536870912 | bytes 12615692 | tf_op jit(solution)/shard_map/vmap(ab,pbc->pac)/dot_general | solution.py:21
  33.5 12.5 %copy.28 = bf16[1,8,2,512,512]{3,4,2,1,0:T(8,128)(2,1)} copy(bf16[1,8,2,512,512]{4,3,2,1,0:T(8,128)(2,1)} %param.9) | data formatting | bytes 16777216 | tf_op args[4]
  46.8 0.1 constant_dynamic-update-slice_fusion.3
  47.0 15.6 %collective-permute-done.3 = bf16[2,4,2,128,128]{4,3,2,1,0:T(8,128)(2,1)S(1)} collective-permute-done((bf16[2,4,2,128,128]{4,3,2,1,0:T(8,128)(2,1)}, bf16[2,4,2,128,128]{4,3,2,1,0:T(8,128)(2,1)S(1)}, u32[]{:S(2)}, u32[]{:S(2)}) %collective-permute-start.3) | collective-permute-done | bytes 524320 | tf_op jit(solution)/shard_map/ppermute | solution.py:13
  62.7 0.1 constant_dynamic-slice_fusion
  62.9 1.1 fusion.17
  64.0 1.2 %fusion.11 = f32[8,128,512,4]{2,1,3,0:T(8,128)S(1)} fusion(bf16[8,2,512,4,128]{2,4,3,1,0:T(8,128)(2,1)S(1)} %bitcast.115, bf16[8,128,128,1]{2,0,1,3:T(8,128)(2,1)S(1)} %get-tuple-element.4), kind=kOutput, calls=%fused_computation.23 | convolution fusion | flops 536870912 | bytes 12845056 | tf_op jit(solution)/shard_map/vmap(ab,iqb->qai)/dot_general | solution.py:34
  65.3 4.4 %fusion.10 = f32[8,128,512,4]{2,1,3,0:T(8,128)} fusion(bf16[8,2,512,4,128]{2,4,3,1,0:T(8,128)(2,1)S(1)} %bitcast.116, bf16[8,128,128,1]{2,0,1,3:T(8,128)(2,1)S(1)} %get-tuple-element.5), kind=kOutput, calls=%fused_computation.22 | convolution fusion | flops 536870912 | bytes 12845056 | tf_op jit(solution)/shard_map/vmap(ab,iqb->qai)/dot_general | solution.py:34
  69.7 4.4 %fusion.4 = f32[8,128,512,4]{2,1,3,0:T(8,128)} fusion(f32[8,128,512,4]{2,1,3,0:T(8,128)S(1)} %fusion.11, bf16[8,2,512,4,128]{2,4,3,1,0:T(8,128)(2,1)S(1)} %bitcast.117, bf16[8,128,128,1]{2,0,1,3:T(8,128)(2,1)S(1)} %get-tuple-element.5), kind=kOutput, calls=%fused_computation.12 | convolution fusion | flops 543162368 | bytes 21233664 | tf_op jit(solution)/shard_map/vmap(ab,iqb->qai)/dot_general | solution.py:34
  74.1 9.1 %copy.33 = f32[8,512,512]{1,2,0:T(8,128)} copy(f32[8,512,512]{2,1,0:T(8,128)} %bitcast.123) | data formatting | bytes 16777216 | tf_op jit(solution)/shard_map/vmap()/transpose | solution.py:48
  83.3 9.1 %fusion.5 = f32[8,128,512,4]{2,1,3,0:T(8,128)} fusion(f32[8,128,512,4]{2,1,3,0:T(8,128)} %fusion.10, bf16[8,2,512,4,128]{2,4,3,1,0:T(8,128)(2,1)} %bitcast.114, bf16[8,128,128,1]{2,0,1,3:T(8,128)(2,1)S(1)} %get-tuple-element.4), kind=kOutput, calls=%fused_computation.13 | convolution fusion | flops 543162368 | bytes 21233664 | tf_op jit(solution)/shard_map/vmap(ab,iqb->qai)/dot_general | solution.py:34
  92.4 9.1 %copy.36 = f32[8,512,512]{1,2,0:T(8,128)} copy(f32[8,512,512]{2,1,0:T(8,128)} %bitcast.122) | data formatting | bytes 16777216 | tf_op jit(solution)/shard_map/vmap()/transpose | solution.py:48
  101.5 12.2 %fusion.1 = (f32[8,512]{1,0:T(8,128)S(1)}, f32[8,512]{1,0:T(8,128)S(1)}) fusion(bf16[128,8,4,512]{3,0,2,1:T(8,128)(2,1)} %subtract_convert_fusion.1, f32[8,512,512]{1,2,0:T(8,128)} %copy.36, f32[8,512,512]{1,2,0:T(8,128)} %copy.33, f32[128,8,4,512]{3,0,2,1:T(8,128)} %fusion.6, bf16[8,2,4,128,512]{4,3,2,0,1:T(8,128)(2,1)} %bitcast.119, ...), kind=kOutput, calls=%fused_computation.3 | convolution fusion | flops 562028544 | bytes 33619976 | tf_op jit(solution)/shard_map/vmap(ab,pbc->pac)/dot_general | solution.py:21
  113.8 0.1 bitcast_reduce_fusion
  113.9 0.6 fusion.24
  114.5 0.6 copy.37
  (20 shorter events, 0.3 us)
Async XLA Ops:
  0.6 46.1 %collective-permute-start = (bf16[2,4,2,128,128]{4,3,2,1,0:T(8,128)(2,1)}, bf16[2,4,2,128,128]{4,3,2,1,0:T(8,128)(2,1)S(1)}, u32[]{:S(2)}, u32[]{:S(2)}) collective-permute-start(bf16[2,4,2,128,128]{4,3,2,1,0:T(8,128)(2,1)} %param.8), channel_id=1, source_target_pairs={{0,14},{2,0},{4,2},{6,4},{8,6},{10,8},{12,10},{14,12},{1,15},{3,1}... | collective-permute-start | bytes 1572872 | tf_op jit(solution)/shard_map/ppermute | solution.py:13
  5.2 41.7 %collective-permute-start.1 = (bf16[2,4,2,128,128]{4,3,2,1,0:T(8,128)(2,1)}, bf16[2,4,2,128,128]{4,3,2,1,0:T(8,128)(2,1)S(1)}, u32[]{:S(2)}, u32[]{:S(2)}) collective-permute-start(bf16[2,4,2,128,128]{4,3,2,1,0:T(8,128)(2,1)} %param.8), channel_id=1, source_target_pairs={{0,12},{2,14},{4,0},{6,2},{8,4},{10,6},{12,8},{14,10},{1,13},{3,15... | collective-permute-start | bytes 1572872 | tf_op jit(solution)/shard_map/ppermute | solution.py:13
  5.8 41.1 %collective-permute-start.2 = (bf16[2,4,2,128,128]{4,3,2,1,0:T(8,128)(2,1)}, bf16[2,4,2,128,128]{4,3,2,1,0:T(8,128)(2,1)S(1)}, u32[]{:S(2)}, u32[]{:S(2)}) collective-permute-start(bf16[2,4,2,128,128]{4,3,2,1,0:T(8,128)(2,1)} %param.8), channel_id=1, source_target_pairs={{0,10},{2,12},{4,14},{6,0},{8,2},{10,4},{12,6},{14,8},{1,11},{3,13... | collective-permute-start | bytes 1572872 | tf_op jit(solution)/shard_map/ppermute | solution.py:13
  5.8 56.8 %collective-permute-start.3 = (bf16[2,4,2,128,128]{4,3,2,1,0:T(8,128)(2,1)}, bf16[2,4,2,128,128]{4,3,2,1,0:T(8,128)(2,1)S(1)}, u32[]{:S(2)}, u32[]{:S(2)}) collective-permute-start(bf16[2,4,2,128,128]{4,3,2,1,0:T(8,128)(2,1)} %param.8), channel_id=1, source_target_pairs={{0,8},{2,10},{4,12},{6,14},{8,0},{10,2},{12,4},{14,6},{1,9},{3,11}... | collective-permute-start | bytes 1572872 | tf_op jit(solution)/shard_map/ppermute | solution.py:13
  11.8 8.1 %copy-start.2 = (bf16[2,4,2,128,128]{4,3,2,1,0:T(8,128)(2,1)S(1)}, bf16[2,4,2,128,128]{4,3,2,1,0:T(8,128)(2,1)}, u32[]{:S(2)}) copy-start(bf16[2,4,2,128,128]{4,3,2,1,0:T(8,128)(2,1)} %param.8) | copy-start | bytes 1572868
  19.8 4.6 %copy-start.1 = (bf16[1,8,2,512,512]{4,3,1,2,0:T(8,128)(2,1)S(1)}, bf16[1,8,2,512,512]{4,3,1,2,0:T(8,128)(2,1)}, u32[]{:S(2)}) copy-start(bf16[1,8,2,512,512]{4,3,1,2,0:T(8,128)(2,1)} %copy.26) | copy-start | bytes 25165828
  27.8 4.5 %copy-start.3 = (s32[8]{0:T(128)S(1)}, s32[8]{0:T(128)}, u32[]{:S(2)}) copy-start(s32[8]{0:T(128)} %param.7) | copy-start | bytes 100
  46.7 17.3 %copy-start = (bf16[1,8,2,512,512]{3,4,2,1,0:T(8,128)(2,1)S(1)}, bf16[1,8,2,512,512]{3,4,2,1,0:T(8,128)(2,1)}, u32[]{:S(2)}) copy-start(bf16[1,8,2,512,512]{3,4,2,1,0:T(8,128)(2,1)} %copy.28) | copy-start | bytes 25165828
where the time goes:
time: 116 us; the launch traced here: 115 us
  matrix products  43.8 us (38%)
  local copies, waits for them, and re-layouts  41.8 us (36%)
  waiting for transfers between devices  15.6 us (13%)
  starting transfers between devices  7.86 us (7%)
  between operations  5.34 us (5%)
    dot_general x4, matrix products, rowmul(): jnp.einsum('ab,pbc->pac', a, b, preferred_element_type=jnp.float32)  23.5 us
    unnamed x14, local copies, waits for them, and re-layouts  21.2 us
    dot_general x4, matrix products, colmul(): jnp.einsum('ab,iqb->qai', a, b, preferred_element_type=jnp.float32)  19.2 us
    transpose x2, local copies, waits for them, and re-layouts, contract(): real_part = jnp.sum(lre * rre.T - lim * rim.T, axis=0)  18.3 us
    ppermute x4, waiting for transfers between devices, from_behind(): return lax.ppermute(value, axis, pairs)  15.6 us
    ppermute x4, starting transfers between devices, from_behind(): return lax.ppermute(value, axis, pairs)  7.86 us
  transfers between devices with their start and end apart: 4, of which 1 were waited for; matrix products, arithmetic and copies ran while one was open for 28% of the time, Pallas kernels for 0%

commit v1 on v0

--- a/solution.py
+++ b/solution.py
@@ -1,6 +1,10 @@
+import functools
+
 import jax
 import jax.numpy as jnp
 from jax import lax
+from jax.experimental import pallas as pl
+from jax.experimental.pallas import tpu as pltpu
 from jax.sharding import PartitionSpec as P
 
 EIG = 128
@@ -75,6 +79,358 @@
     return (terms[None], correlator[None])
 
 
+TILE = 4
+NEAR, FAR = 0, 1
+
+
+def fused_kernel(
+    times_ref,
+    momenta_ref,
+    offsets_ref,
+    elem_ref,
+    tau_ref,
+    terms_ref,
+    corr_ref,
+    tau,
+    own,
+    win,
+    weight,
+    left,
+    outer,
+    tau_sem,
+    own_sem,
+    put_sem,
+    down_send,
+    up_send,
+    relay_send,
+    z_recv,
+    x_send,
+    x_recv,
+    own_send,
+    own_recv,
+    pair_send,
+    pair_recv,
+):
+    src = lax.axis_index("src")
+    x = lax.axis_index("snk")
+    z = lax.div(src, 2)
+    c = lax.rem(src, 2)
+    entries = tau_ref.shape[0]
+    other = 1 - x
+    sibling = {"src": src + 1 - 2 * c}
+    across = {"snk": other}
+
+    def remote(source, target, send, recv, device):
+        return pltpu.make_async_remote_copy(
+            src_ref=source,
+            dst_ref=target,
+            send_sem=send,
+            recv_sem=recv,
+            device_id=device,
+            device_id_type=pl.DeviceIdType.MESH,
+        )
+
+    def place(kind, k):
+        return (2 + 2 * kind + c) * TILE + k
+
+    own_copy = pltpu.make_async_copy(elem_ref, own, own_sem)
+    own_copy.start()
+    put_copy = pltpu.make_async_copy(elem_ref, win.at[:, pl.ds(c * TILE, TILE)], put_sem)
+    put_copy.start()
+    for i in range(entries):
+        pltpu.make_async_copy(tau_ref.at[i], tau.at[i], tau_sem.at[i]).start()
+
+    barrier = pltpu.get_barrier_semaphore()
+
+    def greet(device):
+        pl.semaphore_signal(barrier, inc=1, device_id=device, device_id_type=pl.DeviceIdType.MESH)
+
+    greet(sibling)
+    greet(across)
+    has_up = z <= 1
+
+    @pl.when(z >= 1)
+    def _():
+        greet({"src": src - 2})
+
+    @pl.when(z <= 2)
+    def _():
+        greet({"src": src + 2})
+
+    @pl.when(has_up)
+    def _():
+        greet({"src": src + 4})
+
+    @pl.when(z >= 2)
+    def _():
+        greet({"src": src - 4})
+
+    pl.semaphore_wait(barrier, 4 + jnp.where((z == 1) | (z == 2), 1, 0))
+
+    def down(k):
+        return remote(
+            elem_ref.at[x, k],
+            win.at[x, place(NEAR, k)],
+            down_send.at[k],
+            z_recv.at[NEAR * TILE + k],
+            {"src": src - 2},
+        )
+
+    def up(k):
+        return remote(
+            elem_ref.at[x, k],
+            win.at[x, place(FAR, k)],
+            up_send.at[k],
+            z_recv.at[FAR * TILE + k],
+            {"src": src + 4},
+        )
+
+    @pl.when(z >= 1)
+    def _():
+        for k in range(TILE):
+            down(k).start()
+
+    @pl.when(has_up)
+    def _():
+        for k in range(TILE):
+            up(k).start()
+
+    def own_push():
+        return remote(
+            elem_ref, win.at[:, pl.ds(TILE, TILE)], own_send, own_recv, sibling
+        )
+
+    @pl.when(c == 1)
+    def _():
+        own_push().start()
+
+    def step_of(i):
+        first = z <= 1
+        kind = jnp.where(first, lax.div(i, TILE), lax.rem(i, 2))
+        k = jnp.where(first, lax.rem(i, TILE), lax.div(i, 2))
+        return kind, k
+
+    def arrival(kind, k):
+        slot = win.at[x, place(kind, k)]
+        return remote(slot, slot, x_send.at[0], z_recv.at[kind * TILE + k], across)
+
+    def relay_down(k):
+        return remote(
+            win.at[x, place(NEAR, k)],
+            win.at[x, place(FAR, k)],
+            relay_send.at[NEAR * TILE + k],
+            z_recv.at[FAR * TILE + k],
+            {"src": src - 2},
+        )
+
+    def relay_up(k):
+        return remote(
+            win.at[x, place(FAR, k)],
+            win.at[x, place(NEAR, k)],
+            relay_send.at[FAR * TILE + k],
+            z_recv.at[NEAR * TILE + k],
+            {"src": src + 2},
+        )
+
+    def cross(kind, k, plane):
+        slot = win.at[plane, place(kind, k)]
+        at = kind * TILE + k
+        return remote(slot, slot, x_send.at[at], x_recv.at[at], across)
+
+    def pair(kind, k, plane, hop):
+        slot = win.at[plane, place(kind, k)]
+        at = (hop * 2 + kind) * TILE + k
+        return remote(slot, slot, pair_send.at[at], pair_recv.at[at], sibling)
+
+    def pair_in(kind, k, plane, hop):
+        slot = win.at[plane, (2 + 2 * kind + 1 - c) * TILE + k]
+        at = (hop * 2 + kind) * TILE + k
+        return remote(slot, slot, pair_send.at[at], pair_recv.at[at], sibling)
+
+    own_copy.wait()
+    m0 = momenta_ref[0, 0]
+    m1 = momenta_ref[0, 1]
+    start = lax.rem(times_ref[0], TILE)
+    source = own[m0, start]
+    weight[:EIG, :EIG] = source[0]
+    weight[:EIG, EIG:] = -source[1]
+    weight[EIG:, :EIG] = source[1]
+    weight[EIG:, EIG:] = source[0]
+
+    def hand_on(i):
+        kind, k = step_of(i)
+        arrival(kind, k).wait_recv()
+
+        @pl.when((kind == NEAR) & ((z == 1) | (z == 2)))
+        def _():
+            relay_down(k).start()
+
+        @pl.when((kind == FAR) & (z == 2))
+        def _():
+            relay_up(k).start()
+
+        cross(kind, k, x).start()
+
+        @pl.when((kind == NEAR) | (c == 0))
+        def _():
+            pair(kind, k, x, 0).start()
+
+    def hand_across(i):
+        kind, k = step_of(i)
+        cross(kind, k, other).wait_recv()
+
+        @pl.when((kind == NEAR) | (c == 0))
+        def _():
+            pair(kind, k, other, 1).start()
+
+    def work(i):
+        pltpu.make_async_copy(tau_ref.at[i], tau.at[i], tau_sem.at[i]).wait()
+        for a in range(4):
+            rows = pl.ds(a * EIG, EIG)
+            both = jnp.concatenate([tau[i, 0, rows, :], tau[i, 1, rows, :]], axis=0)
+            product = jnp.dot(weight[...], both, preferred_element_type=jnp.float32)
+            product = product.astype(jnp.bfloat16)
+            left[0, rows, :] = product[:EIG]
+            left[1, rows, :] = product[EIG:]
+        for p in range(4):
+            cols = pl.ds(p * EIG, EIG)
+            t = jnp.concatenate([tau[i, 0, :, cols], tau[i, 1, :, cols]], axis=1)
+            l = jnp.concatenate([left[0, :, cols], left[1, :, cols]], axis=1)
+            q = lax.dot_general(
+                t, l, (((0,), (0,)), ((), ())), preferred_element_type=jnp.float32
+            )
+            outer[i, p, 0] = q[:EIG, :EIG] + q[EIG:, EIG:]
+            outer[i, p, 1] = q[:EIG, EIG:] - q[EIG:, :EIG]
+
+    @pl.loop(0, entries)
+    def _(i):
+        hand_on(i)
+
+        @pl.when(i >= 1)
+        def _():
+            hand_across(i - 1)
+
+        work(i)
+
+    hand_across(entries - 1)
+
+    put_copy.wait()
+
+    @pl.when(c == 0)
+    def _():
+        own_push().wait_recv()
+
+    @pl.when(c == 1)
+    def _():
+        own_push().wait_send()
+
+    for kind in (NEAR, FAR):
+        for k in range(TILE):
+            if kind == NEAR:
+                pair_in(kind, k, x, 0).wait_recv()
+                pair_in(kind, k, other, 1).wait_recv()
+            else:
+
+                @pl.when(c == 1)
+                def _():
+                    pair_in(kind, k, x, 0).wait_recv()
+                    pair_in(kind, k, other, 1).wait_recv()
+
+    def finish(o):
+        sink = win[m1, c * TILE + start + offsets_ref[o]]
+        er = sink[0].astype(jnp.float32).T
+        ei = sink[1].astype(jnp.float32).T
+        for p in range(4):
+            mr = outer[o, p, 0]
+            mi = outer[o, p, 1]
+            cols = pl.ds(p * EIG, EIG)
+            terms_ref[o, 0:1, cols] = jnp.sum(er * mr - ei * mi, axis=0, keepdims=True)
+            terms_ref[o, 1:2, cols] = jnp.sum(er * mi + ei * mr, axis=0, keepdims=True)
+
+    @pl.loop(0, entries)
+    def _(o):
+        finish(o)
+
+    corr_ref[...] = jnp.sum(terms_ref[...], axis=-1) * jnp.float32(ROWS ** (-0.5))
+
+    @pl.when(z >= 1)
+    def _():
+        for k in range(TILE):
+            down(k).wait_send()
+
+    @pl.when(has_up)
+    def _():
+        for k in range(TILE):
+            up(k).wait_send()
+
+    @pl.when((z == 1) | (z == 2))
+    def _():
+        for k in range(TILE):
+            relay_down(k).wait_send()
+
+    @pl.when(z == 2)
+    def _():
+        for k in range(TILE):
+            relay_up(k).wait_send()
+
+    for kind in (NEAR, FAR):
+        for k in range(TILE):
+            cross(kind, k, x).wait_send()
+            if kind == NEAR:
+                pair(kind, k, x, 0).wait_send()
+                pair(kind, k, other, 1).wait_send()
+            else:
+
+                @pl.when(c == 0)
+                def _():
+                    pair(kind, k, x, 0).wait_send()
+                    pair(kind, k, other, 1).wait_send()
+
+
+def fused_local(src_times, momenta, band_offsets, elementals, perambulators):
+    entries = band_offsets.shape[0]
+    bf16 = jnp.bfloat16
+    dma = pltpu.SemaphoreType.DMA
+    smem = pl.BlockSpec(memory_space=pltpu.SMEM)
+    hbm = pl.BlockSpec(memory_space=pl.ANY)
+    vmem = pl.BlockSpec(memory_space=pltpu.VMEM)
+    terms, correlator = pl.pallas_call(
+        fused_kernel,
+        out_shape=(
+            jax.ShapeDtypeStruct((entries, 2, ROWS), jnp.float32),
+            jax.ShapeDtypeStruct((entries, 2), jnp.float32),
+        ),
+        in_specs=[smem, smem, smem, hbm, hbm],
+        out_specs=(vmem, vmem),
+        scratch_shapes=[
+            pltpu.VMEM((entries, 2, ROWS, ROWS), bf16),
+            pltpu.VMEM((2, TILE, 2, EIG, EIG), bf16),
+            pltpu.VMEM((2, 6 * TILE, 2, EIG, EIG), bf16),
+            pltpu.VMEM((2 * EIG, 2 * EIG), bf16),
+            pltpu.VMEM((2, ROWS, ROWS), bf16),
+            pltpu.VMEM((entries, 4, 2, EIG, EIG), jnp.float32),
+            dma((entries,)),
+            dma,
+            dma,
+            dma((TILE,)),
+            dma((TILE,)),
+            dma((2 * TILE,)),
+            dma((2 * TILE,)),
+            dma((2 * TILE,)),
+            dma((2 * TILE,)),
+            dma,
+            dma,
+            dma((4 * TILE,)),
+            dma((4 * TILE,)),
+        ],
+        compiler_params=pltpu.CompilerParams(
+            collective_id=0, has_side_effects=True, vmem_limit_bytes=60 * 1024 * 1024
+        ),
+        name="band_contraction",
+    )(src_times, momenta, band_offsets, elementals, perambulators[0])
+    return terms[None], correlator[None]
+
+
 def solution(mesh):
     placed = (
         P("src"),
@@ -83,8 +439,11 @@
         P("cfg", "src", None, None, None),
         P(("cfg", "src"), "snk", None, None, "spin"),
     )
+    inside = local
+    if dict(mesh.shape) == {"cfg": 2, "src": 8, "snk": 2, "spin": 1}:
+        inside = fused_local
     return jax.shard_map(
-        local,
+        inside,
         mesh=mesh,
         in_specs=placed,
         out_specs=(P(("cfg", "src"), "snk", None, "spin"), P(("cfg", "src"), "snk", None)),

time: 116 us -> 43.1 us (0.37)
  the two profiles are of different devices: /device:TPU:0 before, /device:TPU:25 now
where the time goes in v1:
time: 43.1 us; the launch traced here: 42.8 us
  Pallas kernels  38.9 us (90%)
  local copies, waits for them, and re-layouts  2.69 us (6%)
  between operations  1.28 us (3%)
    pallas_call x1, Pallas kernels, fused_local(): pl.pallas_call(fused_kernel, out_shape=(jax.ShapeDtypeStruct((entries, 2,...  38.9 us
    unnamed x1, local copies, waits for them, and re-layouts  1.37 us
    pallas_call x1, local copies, waits for them, and re-layouts, fused_local(): pl.pallas_call(fused_kernel, out_shape=(jax.ShapeDtypeStruct((entries, 2,...  1.32 us

profile of v1, /device:TPU:25, one launch (start us, length us, event | category | flops | bytes accessed | tf_op | source)
XLA Modules:
  0.0 42.8 jit_solution(7562571552360258134)
XLA Ops:
  1.3 38.9 %band_contraction.1 = (f32[8,2,512]{2,1,0:T(2,128)}, f32[8,2]{1,0:T(8,128)}) custom-call(s32[1]{0:T(128)S(6)} %copy.9.times_ref, s32[1,2]{1,0:T(1,128)} %momenta_ref.1, s32[8]{0:T(128)} %offsets_ref.1, bf16[2,4,2,128,128]{4,3,2,1,0:T(8,128)(2,1)} %elem_ref.1, bf16[8,2,512,512]{3,2,1,0:T(8,128)(2,1)} %bitcast.3), custom_call_target="tpu_custom_call" | custom-call | tf_op jit(solution)/shard_map/band_contraction/pallas_call | solution.py:397
  40.2 1.3 %copy.7 = f32[8,2]{0,1:T(2,128)} copy(f32[8,2]{1,0:T(8,128)} %get-tuple-element.5) | data formatting | bytes 128 | tf_op jit(solution)/shard_map/band_contraction/pallas_call | solution.py:397
  41.5 1.4 %copy.10 = f32[1,8,2,512]{3,2,1,0:T(2,128)} copy(f32[1,8,2,512]{3,2,1,0:T(2,128)} %bitcast.4) | data formatting | bytes 65536

commit v2 on v1

--- a/solution.py
+++ b/solution.py
@@ -165,8 +165,6 @@
     def _():
         greet({"src": src - 4})
 
-    pl.semaphore_wait(barrier, 4 + jnp.where((z == 1) | (z == 2), 1, 0))
-
     def down(k):
         return remote(
             elem_ref.at[x, k],
@@ -185,30 +183,82 @@
             {"src": src + 4},
         )
 
-    @pl.when(z >= 1)
-    def _():
-        for k in range(TILE):
-            down(k).start()
-
-    @pl.when(has_up)
-    def _():
-        for k in range(TILE):
-            up(k).start()
-
     def own_push():
         return remote(
             elem_ref, win.at[:, pl.ds(TILE, TILE)], own_send, own_recv, sibling
         )
 
-    @pl.when(c == 1)
-    def _():
-        own_push().start()
-
     def step_of(i):
         first = z <= 1
-        kind = jnp.where(first, lax.div(i, TILE), lax.rem(i, 2))
+        odd = lax.rem(i + jnp.where(z == 2, 1, 0), 2)
+        kind = jnp.where(first, lax.div(i, TILE), odd)
         k = jnp.where(first, lax.rem(i, TILE), lax.div(i, 2))
         return kind, k
+
+    def wanted(kind, k):
+        return (kind == NEAR) | (k < TILE - 1) | (c == 0)
+
+    def feed(i):
+        @pl.when((z == 1) | (z == 2))
+        def _():
+            @pl.when(i == 0)
+            def _():
+                down(0).start()
+                down(1).start()
+
+            @pl.when(i == 1)
+            def _():
+                down(2).start()
+
+            @pl.when(i == 2)
+            def _():
+                down(3).start()
+
+        @pl.when(z == 0)
+        def _():
+            @pl.when(i == 0)
+            def _():
+                up(0).start()
+                up(1).start()
+
+            @pl.when(i == 1)
+            def _():
+                up(2).start()
+
+            @pl.when(i == 2)
+            def _():
+                up(3).start()
+
+        @pl.when(z == 1)
+        def _():
+            @pl.when(i == 3)
+            def _():
+                relay_down(0).start()
+                up(0).start()
+
+            @pl.when(i == 4)
+            def _():
+                relay_down(1).start()
+                relay_down(2).start()
+                up(1).start()
+
+            @pl.when(i == 5)
+            def _():
+                up(2).start()
+
+                @pl.when(c == 0)
+                def _():
+                    relay_down(3).start()
+                    up(3).start()
+
+        @pl.when((z == 3) & (i == 0))
+        def _():
+            down(0).start()
+            down(1).start()
+            down(0).wait_send()
+            down(2).start()
+            down(1).wait_send()
+            down(3).start()
 
     def arrival(kind, k):
         slot = win.at[x, place(kind, k)]
@@ -259,9 +309,12 @@
 
     def hand_on(i):
         kind, k = step_of(i)
-        arrival(kind, k).wait_recv()
-
-        @pl.when((kind == NEAR) & ((z == 1) | (z == 2)))
+
+        @pl.when((kind == NEAR) | (k < TILE - 1) | (c == 0) | (z == 2))
+        def _():
+            arrival(kind, k).wait_recv()
+
+        @pl.when((kind == NEAR) & (z == 2) & ((c == 0) | (k < TILE - 1)))
         def _():
             relay_down(k).start()
 
@@ -269,7 +322,9 @@
         def _():
             relay_up(k).start()
 
-        cross(kind, k, x).start()
+        @pl.when(wanted(kind, k))
+        def _():
+            cross(kind, k, x).start()
 
         @pl.when((kind == NEAR) | (c == 0))
         def _():
@@ -277,7 +332,10 @@
 
     def hand_across(i):
         kind, k = step_of(i)
-        cross(kind, k, other).wait_recv()
+
+        @pl.when(wanted(kind, k))
+        def _():
+            cross(kind, k, other).wait_recv()
 
         @pl.when((kind == NEAR) | (c == 0))
         def _():
@@ -302,15 +360,31 @@
             outer[i, p, 0] = q[:EIG, :EIG] + q[EIG:, EIG:]
             outer[i, p, 1] = q[:EIG, EIG:] - q[EIG:, :EIG]
 
+    early = jnp.where(z == 0, 3, jnp.where(z == 1, 1, 0))
+
+    @pl.loop(0, early)
+    def _(i):
+        work(i)
+
+    pl.semaphore_wait(barrier, 4 + jnp.where((z == 1) | (z == 2), 1, 0))
+
     @pl.loop(0, entries)
     def _(i):
+        feed(i)
+
+        @pl.when((c == 1) & (i == 0))
+        def _():
+            own_push().start()
+
         hand_on(i)
 
         @pl.when(i >= 1)
         def _():
             hand_across(i - 1)
 
-        work(i)
+        @pl.when(early + i < entries)
+        def _():
+            work(early + i)
 
     hand_across(entries - 1)
 
@@ -353,29 +427,38 @@
 
     corr_ref[...] = jnp.sum(terms_ref[...], axis=-1) * jnp.float32(ROWS ** (-0.5))
 
-    @pl.when(z >= 1)
+    @pl.when((z == 1) | (z == 2))
     def _():
         for k in range(TILE):
             down(k).wait_send()
 
-    @pl.when(has_up)
-    def _():
-        for k in range(TILE):
+    @pl.when(z == 3)
+    def _():
+        down(2).wait_send()
+        down(3).wait_send()
+
+    for k in range(TILE):
+        last = k == TILE - 1
+
+        @pl.when((z == 0) | ((z == 1) & ((c == 0) | (not last))))
+        def _():
             up(k).wait_send()
 
-    @pl.when((z == 1) | (z == 2))
-    def _():
-        for k in range(TILE):
+        @pl.when(((z == 1) | (z == 2)) & ((c == 0) | (not last)))
+        def _():
             relay_down(k).wait_send()
 
-    @pl.when(z == 2)
-    def _():
-        for k in range(TILE):
+        @pl.when(z == 2)
+        def _():
             relay_up(k).wait_send()
 
     for kind in (NEAR, FAR):
         for k in range(TILE):
-            cross(kind, k, x).wait_send()
+
+            @pl.when(wanted(kind, k))
+            def _():
+                cross(kind, k, x).wait_send()
+
             if kind == NEAR:
                 pair(kind, k, x, 0).wait_send()
                 pair(kind, k, other, 1).wait_send()

time: 43.1 us -> 44.1 us (1.023)
  the two profiles are of different devices: /device:TPU:25 before, /device:TPU:31 now
where the time goes in v2:
time: 44.1 us; the launch traced here: 43.8 us
  Pallas kernels  39.9 us (90%)
  local copies, waits for them, and re-layouts  2.69 us (6%)
  between operations  1.28 us (3%)
    pallas_call x1, Pallas kernels, fused_local(): pl.pallas_call(fused_kernel, out_shape=(jax.ShapeDtypeStruct((entries, 2,...  39.9 us
    unnamed x1, local copies, waits for them, and re-layouts  1.37 us
    pallas_call x1, local copies, waits for them, and re-layouts, fused_local(): pl.pallas_call(fused_kernel, out_shape=(jax.ShapeDtypeStruct((entries, 2,...  1.32 us

profile of v2, /device:TPU:31, one launch (start us, length us, event | category | flops | bytes accessed | tf_op | source)
XLA Modules:
  0.0 43.8 jit_solution(12031432471644458770)
XLA Ops:
  1.3 39.9 %band_contraction.1 = (f32[8,2,512]{2,1,0:T(2,128)}, f32[8,2]{1,0:T(8,128)}) custom-call(s32[1]{0:T(128)S(6)} %copy.9.times_ref, s32[1,2]{1,0:T(1,128)} %momenta_ref.1, s32[8]{0:T(128)} %offsets_ref.1, bf16[2,4,2,128,128]{4,3,2,1,0:T(8,128)(2,1)} %elem_ref.1, bf16[8,2,512,512]{3,2,1,0:T(8,128)(2,1)} %bitcast.3), custom_call_target="tpu_custom_call" | custom-call | tf_op jit(solution)/shard_map/band_contraction/pallas_call | solution.py:480
  41.2 1.3 %copy.7 = f32[8,2]{0,1:T(2,128)} copy(f32[8,2]{1,0:T(8,128)} %get-tuple-element.5) | data formatting | bytes 128 | tf_op jit(solution)/shard_map/band_contraction/pallas_call | solution.py:480
  42.5 1.4 %copy.10 = f32[1,8,2,512]{3,2,1,0:T(2,128)} copy(f32[1,8,2,512]{3,2,1,0:T(2,128)} %bitcast.4) | data formatting | bytes 65536

commit v3 on v1

--- a/solution.py
+++ b/solution.py
@@ -165,8 +165,6 @@
     def _():
         greet({"src": src - 4})
 
-    pl.semaphore_wait(barrier, 4 + jnp.where((z == 1) | (z == 2), 1, 0))
-
     def down(k):
         return remote(
             elem_ref.at[x, k],
@@ -185,30 +183,57 @@
             {"src": src + 4},
         )
 
-    @pl.when(z >= 1)
-    def _():
-        for k in range(TILE):
-            down(k).start()
-
-    @pl.when(has_up)
-    def _():
-        for k in range(TILE):
-            up(k).start()
-
     def own_push():
         return remote(
             elem_ref, win.at[:, pl.ds(TILE, TILE)], own_send, own_recv, sibling
         )
 
-    @pl.when(c == 1)
-    def _():
-        own_push().start()
-
     def step_of(i):
         first = z <= 1
-        kind = jnp.where(first, lax.div(i, TILE), lax.rem(i, 2))
-        k = jnp.where(first, lax.rem(i, TILE), lax.div(i, 2))
+        odd = lax.rem(lax.div(i, 2) + jnp.where(z == 2, 1, 0), 2)
+        kind = jnp.where(first, lax.div(i, TILE), odd)
+        k = jnp.where(first, lax.rem(i, TILE), lax.div(i, TILE) * 2 + lax.rem(i, 2))
         return kind, k
+
+    def wanted(kind, k):
+        return (kind == NEAR) | (k < TILE - 1) | (c == 0)
+
+    def first_batch():
+        for k in (0, 1):
+
+            @pl.when(z >= 1)
+            def _():
+                down(k).start()
+
+            @pl.when(z == 0)
+            def _():
+                up(k).start()
+
+    def second_batch():
+        for k in (0, 1):
+
+            @pl.when(z >= 1)
+            def _():
+                down(k).wait_send()
+                down(k + 2).start()
+
+            @pl.when(z == 0)
+            def _():
+                up(k).wait_send()
+                up(k + 2).start()
+
+            @pl.when(z == 1)
+            def _():
+                up(k).start()
+
+    def third_batch():
+        up(0).wait_send()
+        up(2).start()
+        up(1).wait_send()
+
+        @pl.when(c == 0)
+        def _():
+            up(3).start()
 
     def arrival(kind, k):
         slot = win.at[x, place(kind, k)]
@@ -259,9 +284,12 @@
 
     def hand_on(i):
         kind, k = step_of(i)
-        arrival(kind, k).wait_recv()
-
-        @pl.when((kind == NEAR) & ((z == 1) | (z == 2)))
+
+        @pl.when((kind == NEAR) | (k < TILE - 1) | (c == 0) | (z == 2))
+        def _():
+            arrival(kind, k).wait_recv()
+
+        @pl.when((kind == NEAR) & ((z == 1) | (z == 2)) & ((c == 0) | (k < TILE - 1)))
         def _():
             relay_down(k).start()
 
@@ -269,7 +297,9 @@
         def _():
             relay_up(k).start()
 
-        cross(kind, k, x).start()
+        @pl.when(wanted(kind, k))
+        def _():
+            cross(kind, k, x).start()
 
         @pl.when((kind == NEAR) | (c == 0))
         def _():
@@ -277,7 +307,10 @@
 
     def hand_across(i):
         kind, k = step_of(i)
-        cross(kind, k, other).wait_recv()
+
+        @pl.when(wanted(kind, k))
+        def _():
+            cross(kind, k, other).wait_recv()
 
         @pl.when((kind == NEAR) | (c == 0))
         def _():
@@ -302,16 +335,45 @@
             outer[i, p, 0] = q[:EIG, :EIG] + q[EIG:, EIG:]
             outer[i, p, 1] = q[:EIG, EIG:] - q[EIG:, :EIG]
 
+    early = jnp.where(z == 0, 3, jnp.where(z == 1, 1, 0))
+
+    @pl.loop(0, early)
+    def _(i):
+        work(i)
+
+    pl.semaphore_wait(barrier, 4 + jnp.where((z == 1) | (z == 2), 1, 0))
+
+    first_batch()
+
+    @pl.when(c == 1)
+    def _():
+        own_push().start()
+
+    work(early)
+    second_batch()
+    ahead = early + 1 + jnp.where(z == 3, 3, 0)
+
+    @pl.loop(early + 1, ahead)
+    def _(i):
+        work(i)
+
     @pl.loop(0, entries)
     def _(i):
         hand_on(i)
 
-        @pl.when(i >= 1)
-        def _():
-            hand_across(i - 1)
-
-        work(i)
-
+        @pl.when((z == 1) & (i == 1))
+        def _():
+            third_batch()
+
+        @pl.when(i >= 2)
+        def _():
+            hand_across(i - 2)
+
+        @pl.when(ahead + i < entries)
+        def _():
+            work(ahead + i)
+
+    hand_across(entries - 2)
     hand_across(entries - 1)
 
     put_copy.wait()
@@ -355,27 +417,35 @@
 
     @pl.when(z >= 1)
     def _():
-        for k in range(TILE):
-            down(k).wait_send()
-
-    @pl.when(has_up)
-    def _():
-        for k in range(TILE):
-            up(k).wait_send()
-
-    @pl.when((z == 1) | (z == 2))
-    def _():
-        for k in range(TILE):
+        down(2).wait_send()
+        down(3).wait_send()
+
+    @pl.when(z <= 1)
+    def _():
+        up(2).wait_send()
+
+    @pl.when((z == 0) | ((z == 1) & (c == 0)))
+    def _():
+        up(3).wait_send()
+
+    for k in range(TILE):
+        last = k == TILE - 1
+
+        @pl.when(((z == 1) | (z == 2)) & ((c == 0) | (not last)))
+        def _():
             relay_down(k).wait_send()
 
-    @pl.when(z == 2)
-    def _():
-        for k in range(TILE):
+        @pl.when(z == 2)
+        def _():
             relay_up(k).wait_send()
 
     for kind in (NEAR, FAR):
         for k in range(TILE):
-            cross(kind, k, x).wait_send()
+
+            @pl.when(wanted(kind, k))
+            def _():
+                cross(kind, k, x).wait_send()
+
             if kind == NEAR:
                 pair(kind, k, x, 0).wait_send()
                 pair(kind, k, other, 1).wait_send()

time: 43.1 us -> 39.3 us (0.912)
  Pallas kernels: 38.9 us -> 35.1 us
    pallas_call x1, Pallas kernels: 38.9 us -> 35.1 us  [fused_local(): pl.pallas_call(fused_kernel, out_shape=(jax.ShapeDtypeStruct((entries, 2,...]
where the time goes in v3:
time: 39.3 us; the launch traced here: 39.1 us
  Pallas kernels  35.1 us (89%)
  local copies, waits for them, and re-layouts  2.69 us (7%)
  between operations  1.28 us (3%)
    pallas_call x1, Pallas kernels, fused_local(): pl.pallas_call(fused_kernel, out_shape=(jax.ShapeDtypeStruct((entries, 2,...  35.1 us
    unnamed x1, local copies, waits for them, and re-layouts  1.37 us
    pallas_call x1, local copies, waits for them, and re-layouts, fused_local(): pl.pallas_call(fused_kernel, out_shape=(jax.ShapeDtypeStruct((entries, 2,...  1.32 us

profile of v3, /device:TPU:25, one launch (start us, length us, event | category | flops | bytes accessed | tf_op | source)
XLA Modules:
  0.0 39.1 jit_solution(7920252188393595849)
XLA Ops:
  1.3 35.1 %band_contraction.1 = (f32[8,2,512]{2,1,0:T(2,128)}, f32[8,2]{1,0:T(8,128)}) custom-call(s32[1]{0:T(128)S(6)} %copy.9.times_ref, s32[1,2]{1,0:T(1,128)} %momenta_ref.1, s32[8]{0:T(128)} %offsets_ref.1, bf16[2,4,2,128,128]{4,3,2,1,0:T(8,128)(2,1)} %elem_ref.1, bf16[8,2,512,512]{3,2,1,0:T(8,128)(2,1)} %bitcast.3), custom_call_target="tpu_custom_call" | custom-call | tf_op jit(solution)/shard_map/band_contraction/pallas_call | solution.py:467
  36.4 1.3 %copy.7 = f32[8,2]{0,1:T(2,128)} copy(f32[8,2]{1,0:T(8,128)} %get-tuple-element.5) | data formatting | bytes 128 | tf_op jit(solution)/shard_map/band_contraction/pallas_call | solution.py:467
  37.7 1.4 %copy.10 = f32[1,8,2,512]{3,2,1,0:T(2,128)} copy(f32[1,8,2,512]{3,2,1,0:T(2,128)} %bitcast.4) | data formatting | bytes 65536

commit v4 on v3

--- a/solution.py
+++ b/solution.py
@@ -190,7 +190,7 @@
 
     def step_of(i):
         first = z <= 1
-        odd = lax.rem(lax.div(i, 2) + jnp.where(z == 2, 1, 0), 2)
+        odd = lax.rem(lax.div(i, 2) + jnp.where(z == 3, 1, 0), 2)
         kind = jnp.where(first, lax.div(i, TILE), odd)
         k = jnp.where(first, lax.rem(i, TILE), lax.div(i, TILE) * 2 + lax.rem(i, 2))
         return kind, k
@@ -205,7 +205,7 @@
             def _():
                 down(k).start()
 
-            @pl.when(z == 0)
+            @pl.when(z <= 1)
             def _():
                 up(k).start()
 
@@ -221,10 +221,6 @@
             def _():
                 up(k).wait_send()
                 up(k + 2).start()
-
-            @pl.when(z == 1)
-            def _():
-                up(k).start()
 
     def third_batch():
         up(0).wait_send()
@@ -351,7 +347,7 @@
 
     work(early)
     second_batch()
-    ahead = early + 1 + jnp.where(z == 3, 3, 0)
+    ahead = early + 1 + jnp.where(z == 3, 5, 0)
 
     @pl.loop(early + 1, ahead)
     def _(i):

time: 39.3 us -> 36.2 us (0.921)
  Pallas kernels: 35.1 us -> 32 us
    pallas_call x1, Pallas kernels: 35.1 us -> 32 us  [fused_local(): pl.pallas_call(fused_kernel, out_shape=(jax.ShapeDtypeStruct((entries, 2,...]
where the time goes in v4:
time: 36.2 us; the launch traced here: 36 us
  Pallas kernels  32 us (88%)
  local copies, waits for them, and re-layouts  2.69 us (7%)
  between operations  1.28 us (4%)
    pallas_call x1, Pallas kernels, fused_local(): pl.pallas_call(fused_kernel, out_shape=(jax.ShapeDtypeStruct((entries, 2,...  32 us
    unnamed x1, local copies, waits for them, and re-layouts  1.37 us
    pallas_call x1, local copies, waits for them, and re-layouts, fused_local(): pl.pallas_call(fused_kernel, out_shape=(jax.ShapeDtypeStruct((entries, 2,...  1.32 us

profile of v4, /device:TPU:25, one launch (start us, length us, event | category | flops | bytes accessed | tf_op | source)
XLA Modules:
  0.0 36.0 jit_solution(1994842967323000179)
XLA Ops:
  1.3 32.0 %band_contraction.1 = (f32[8,2,512]{2,1,0:T(2,128)}, f32[8,2]{1,0:T(8,128)}) custom-call(s32[1]{0:T(128)S(6)} %copy.9.times_ref, s32[1,2]{1,0:T(1,128)} %momenta_ref.1, s32[8]{0:T(128)} %offsets_ref.1, bf16[2,4,2,128,128]{4,3,2,1,0:T(8,128)(2,1)} %elem_ref.1, bf16[8,2,512,512]{3,2,1,0:T(8,128)(2,1)} %bitcast.3), custom_call_target="tpu_custom_call" | custom-call | tf_op jit(solution)/shard_map/band_contraction/pallas_call | solution.py:463
  33.3 1.3 %copy.7 = f32[8,2]{0,1:T(2,128)} copy(f32[8,2]{1,0:T(8,128)} %get-tuple-element.5) | data formatting | bytes 128 | tf_op jit(solution)/shard_map/band_contraction/pallas_call | solution.py:463
  34.6 1.4 %copy.10 = f32[1,8,2,512]{3,2,1,0:T(2,128)} copy(f32[1,8,2,512]{3,2,1,0:T(2,128)} %bitcast.4) | data formatting | bytes 65536
